TPU v7x, 128 devices: a whole 4x4x4 slice. The times are simulated.
128 devices in a mesh: dev: 128 (over z, y, x, core).
Axes of the slice: x: 4, y: 4, z: 4, core: 2. Of those that a mesh axis runs over, the one named last changes fastest.
Arguments:
- pose_input: bfloat16 [16384, 256], P('dev'), may hold values from -6 to 6
- w_in: bfloat16 [256, 1024], replicated, may hold values from -0.375 to 0.375
- w_hid: bfloat16 [1024, 1024], replicated, may hold values from -0.1875 to 0.1875
- w_out: bfloat16 [1024, 256], replicated, may hold values from -0.1875 to 0.1875
- targets: bfloat16 [16384, 15744], P('dev'), may hold values from -6 to 6
- basis: bfloat16 [128, 256, 15744], P('dev'), may hold values from -0.375 to 0.375
- owner: int32 [128], replicated, may hold values from 0 to 127, each once
- frame_subject: int32 [16384, 1], P('dev'), may hold values from 0 to 127; in each aligned block of 128 rows (0 to 127, 128 to 255, ...) at most 2 rows name the same one
Outputs:
- grad_w_in: float32 [256, 1024], P(None, 'dev')
- grad_w_hid: float32 [1024, 1024], P('dev')
- grad_w_out: float32 [1024, 256], P('dev')
- grad_basis: bfloat16 [128, 256, 15744], P('dev')
Inputs may be any that keep to these rules, and one draw needn't show every extreme that they name: owner is a permutation: each slot holds exactly one subject. `frame_subject`: among the 128 frames of one device no subject appears more than 2 times.
All inputs are finite; a program needn't handle non-finite values.
Results may differ from a plain program's by a relative error of at most 0.0063.
Values may be sent and summed in bfloat16 or wider, within the bound.
A program may use at most 128 MiB of HBM per device.

v0:
```python
import jax
import jax.numpy as jnp
from jax import lax
from jax.sharding import PartitionSpec as P


def silu_slope(value):
    sig = jax.nn.sigmoid(value)
    return sig * (1.0 + value * (1.0 - sig))


def inner_rows(left, right):
    return lax.dot_general(
        left, right, (((0,), (0,)), ((), ())), preferred_element_type=jnp.float32
    )


def inner_cols(left, right):
    return lax.dot_general(
        left, right, (((1,), (1,)), ((), ())), preferred_element_type=jnp.float32
    )


def on_device(pose_input, w_in, w_hid, w_out, targets, basis, owner, frame_subject):
    devices = lax.axis_size("dev")
    frames_here = pose_input.shape[0]
    capacity = max(2, 2 * frames_here // devices)
    pre_one = jnp.dot(pose_input, w_in, preferred_element_type=jnp.float32)
    hidden_one = jax.nn.silu(pre_one).astype(jnp.bfloat16)
    pre_two = jnp.dot(hidden_one, w_hid, preferred_element_type=jnp.float32)
    hidden_two = jax.nn.silu(pre_two).astype(jnp.bfloat16)
    features = jnp.dot(hidden_two, w_out, preferred_element_type=jnp.float32).astype(jnp.bfloat16)
    feat_width = features.shape[1]
    vert_width = targets.shape[1]
    scale = vert_width ** (-0.5)
    subject = frame_subject[:, 0]
    subject_ids = jnp.arange(owner.shape[0], dtype=jnp.int32)
    dest_slot = jnp.sum(
        jnp.where(subject[:, None] == subject_ids[None, :], owner[None, :], 0), axis=1
    )
    slot_ids = jnp.arange(devices, dtype=jnp.int32)
    onehot = (dest_slot[:, None] == slot_ids[None, :]).astype(jnp.int32)
    running = jnp.cumsum(onehot, axis=0)
    rank_in = jnp.sum(onehot * (running - 1), axis=1)
    slot_row = dest_slot * capacity + rank_in
    send_feat = jnp.zeros((devices * capacity, feat_width), jnp.bfloat16).at[slot_row].set(features)
    send_target = (
        jnp.zeros((devices * capacity, vert_width), jnp.bfloat16).at[slot_row].set(targets)
    )
    local_basis = basis[0]
    got_feat, got_target = (
        lax.all_to_all(send_feat, "dev", split_axis=0, concat_axis=0, tiled=True),
        lax.all_to_all(send_target, "dev", split_axis=0, concat_axis=0, tiled=True),
    )
    predicted = jnp.dot(got_feat, local_basis, preferred_element_type=jnp.float32)
    grad_corr = ((predicted - got_target.astype(jnp.float32)) * scale).astype(jnp.bfloat16)
    grad_back = inner_cols(grad_corr, local_basis).astype(jnp.bfloat16)
    returned = lax.all_to_all(grad_back, "dev", split_axis=0, concat_axis=0, tiled=True)
    grad_basis = inner_rows(got_feat, grad_corr).astype(jnp.bfloat16)[None]
    grad_feat = returned[slot_row]
    grad_wout = inner_rows(hidden_two, grad_feat)
    back_two = (inner_cols(grad_feat, w_out) * silu_slope(pre_two)).astype(jnp.bfloat16)
    grad_whid = inner_rows(hidden_one, back_two)
    back_one = (inner_cols(back_two, w_hid) * silu_slope(pre_one)).astype(jnp.bfloat16)
    grad_win = inner_rows(pose_input, back_one)
    totals = lax.psum((grad_win, grad_whid, grad_wout), "dev")
    width_share = grad_whid.shape[0] // devices
    start = lax.axis_index("dev") * width_share
    out_win = lax.dynamic_slice_in_dim(totals[0], start, width_share, 1)
    out_whid = lax.dynamic_slice_in_dim(totals[1], start, width_share, 0)
    out_wout = lax.dynamic_slice_in_dim(totals[2], start, width_share, 0)
    return (out_win, out_whid, out_wout, grad_basis)


def solution(mesh):
    in_specs = (
        P("dev", None),
        P(),
        P(),
        P(),
        P("dev", None),
        P("dev", None, None),
        P(),
        P("dev", None),
    )
    out_specs = (P(None, "dev"), P("dev", None), P("dev", None), P("dev", None, None))
    return jax.shard_map(
        on_device, mesh=mesh, in_specs=in_specs, out_specs=out_specs, check_vma=False
    )
```

profile of v0, /device:TPU:1, one launch (start us, length us, event | category | flops | bytes accessed | tf_op | source)
XLA Modules:
  0.0 389.5 jit_solution(9168915967513068420)
XLA Ops:
  7.2 1.0 select_reduce_fusion.1
  8.6 1.3 fusion.26
  11.2 1.3 convolution_convert_fusion.1
  12.5 1.1 scatter_custom_fusion
  14.3 11.5 %all-to-all-start = ((bf16[128,2,256]{2,1,0:T(2,128)(2,1)}), bf16[128,2,256]{2,1,0:T(2,128)(2,1)S(1)}, u32[]{:S(2)}, u32[]{:S(2)}) async-start(bf16[128,2,256]{2,1,0:T(2,128)(2,1)} %all_to_all.22), calls=%async_computation | async-start | bytes 262144 | tf_op jit(solution)/shard_map/all_to_all | solution.py:52
  25.8 12.0 %scatter_custom_fusion.1 = bf16[256,15744]{1,0:T(8,128)(2,1)} fusion(s32[128]{0:T(128)S(1)} %fusion.21, bf16[128,15744]{1,0:T(8,128)(2,1)} %param.12, bf16[]{:T(256)} %constant.10.clone.1), kind=kCustom, calls=%fused_computation.11 | custom fusion | bytes 8061440 | tf_op jit(solution)/shard_map/scatter | solution.py:48
  37.8 14.8 %all_to_all.25 = bf16[128,2,15744]{2,1,0:T(2,128)(2,1)} reshape(bf16[256,15744]{1,0:T(8,128)(2,1)} %scatter_custom_fusion.1) | data formatting | bytes 16121856 | tf_op jit(solution)/shard_map/all_to_all | solution.py:53
  52.6 10.2 %all-to-all-start.1 = ((bf16[128,2,15744]{2,1,0:T(2,128)(2,1)}), bf16[128,2,15744]{2,1,0:T(2,128)(2,1)}, u32[]{:S(2)}, u32[]{:S(2)}) async-start(bf16[128,2,15744]{2,1,0:T(2,128)(2,1)} %all_to_all.25), calls=%async_computation.1 | async-start | bytes 16121856 | tf_op jit(solution)/shard_map/all_to_all | solution.py:53
  62.8 94.9 %all-to-all-done.1 = bf16[128,2,15744]{2,1,0:T(2,128)(2,1)} async-done(((bf16[128,2,15744]{2,1,0:T(2,128)(2,1)}), bf16[128,2,15744]{2,1,0:T(2,128)(2,1)}, u32[]{:S(2)}, u32[]{:S(2)}) %all-to-all-start.1) | async-done | bytes 8060960 | tf_op jit(solution)/shard_map/all_to_all | solution.py:53
  157.7 16.3 %reshape.44 = f32[256,15744]{1,0:T(8,128)} reshape(bf16[128,2,15744]{2,1,0:T(2,128)(2,1)} %all-to-all-done.1) | data formatting | bytes 24182784 | tf_op jit(solution)/shard_map/convert_element_type | solution.py:56
  174.0 11.1 %fusion.1 = bf16[256,15744]{1,0:T(8,128)(2,1)} fusion(f32[256,15744]{1,0:T(8,128)} %reshape.44, bf16[256,256]{1,0:T(8,128)(2,1)S(1)} %all_to_all.24, bf16[1,256,15744]{2,1,0:T(8,128)(2,1)} %param.13), kind=kOutput, calls=%fused_computation.5 | convolution fusion | flops 2075688960 | bytes 32374784 | tf_op jit(solution)/shard_map/dot_general | solution.py:55
  185.2 7.9 %fusion.10 = bf16[256,256]{1,0:T(8,128)(2,1)S(1)} fusion(bf16[256,15744]{1,0:T(8,128)(2,1)} %fusion.1, bf16[1,256,15744]{2,1,0:T(8,128)(2,1)} %param.13), kind=kOutput, calls=%fused_computation.18 | convolution fusion | flops 2063663104 | bytes 16252928 | tf_op jit(solution)/shard_map/dot_general | solution.py:19
  193.8 10.3 %all-to-all-start.2 = ((bf16[128,2,256]{2,1,0:T(2,128)(2,1)}), bf16[128,2,256]{2,1,0:T(2,128)(2,1)S(1)}, u32[]{:S(2)}, u32[]{:S(2)}) async-start(bf16[128,2,256]{2,1,0:T(2,128)(2,1)} %all_to_all.27), calls=%async_computation.2 | async-start | bytes 262144 | tf_op jit(solution)/shard_map/all_to_all | solution.py:58
  204.3 9.7 %all-to-all-done.2 = bf16[128,2,256]{2,1,0:T(2,128)(2,1)S(1)} async-done(((bf16[128,2,256]{2,1,0:T(2,128)(2,1)}), bf16[128,2,256]{2,1,0:T(2,128)(2,1)S(1)}, u32[]{:S(2)}, u32[]{:S(2)}) %all-to-all-start.2) | async-done | bytes 131104 | tf_op jit(solution)/shard_map/all_to_all | solution.py:58
  214.1 0.8 gather_fusion
  215.0 1.5 fusion.8
  216.5 2.7 fusion.23
  219.2 2.2 convolution_bitcast_fusion
  221.4 2.4 fusion.25
  223.8 8.9 %fusion.2 = bf16[1,256,15744]{2,1,0:T(8,128)(2,1)} fusion(bf16[256,256]{1,0:T(8,128)(2,1)S(1)} %all_to_all.24, bf16[256,15744]{1,0:T(8,128)(2,1)} %fusion.1), kind=kOutput, calls=%fused_computation.7 | convolution fusion | flops 2067628032 | bytes 16252928 | tf_op jit(solution)/shard_map/dot_general | solution.py:13
  232.7 146.0 %all-reduce.3.cloned.1.call-done = (f32[256,1024]{0,1:T(8,128)}, f32[1024,1024]{1,0:T(8,128)}, f32[1024,256]{1,0:T(8,128)}) async-done(((f32[256,1024]{0,1:T(8,128)}, f32[1024,1024]{1,0:T(8,128)}, f32[1024,256]{1,0:T(8,128)}), (f32[256,1024]{0,1:T(8,128)}, f32[1024,1024]{1,0:T(8,128)}, f32[1024,256]{1,0:T(8,128)})) %all-reduce.3.cloned.1.call-update) | async-done | bytes 6291472 | tf_op jit(solution)/shard_map/psum | solution.py:66
  378.7 1.4 constant_dynamic-slice_fusion
  380.0 1.3 constant_dynamic-slice_fusion.2
  381.3 1.3 constant_dynamic-slice_fusion.1
  (19 shorter events, 3.5 us)
Async XLA Ops:
  7.2 2.8 copy-start
  10.4 0.8 copy-start.2
  14.3 38.3 %all-to-all-start = ((bf16[128,2,256]{2,1,0:T(2,128)(2,1)}), bf16[128,2,256]{2,1,0:T(2,128)(2,1)S(1)}, u32[]{:S(2)}, u32[]{:S(2)}) async-start(bf16[128,2,256]{2,1,0:T(2,128)(2,1)} %all_to_all.22), calls=%async_computation | async-start | bytes 262144 | tf_op jit(solution)/shard_map/all_to_all | solution.py:52
  52.6 105.1 %all-to-all-start.1 = ((bf16[128,2,15744]{2,1,0:T(2,128)(2,1)}), bf16[128,2,15744]{2,1,0:T(2,128)(2,1)}, u32[]{:S(2)}, u32[]{:S(2)}) async-start(bf16[128,2,15744]{2,1,0:T(2,128)(2,1)} %all_to_all.25), calls=%async_computation.1 | async-start | bytes 16121856 | tf_op jit(solution)/shard_map/all_to_all | solution.py:53
  193.0 26.2 %copy-start.1 = (bf16[128,256]{1,0:T(8,128)(2,1)S(1)}, bf16[128,256]{1,0:T(8,128)(2,1)}, u32[]{:S(2)}) copy-start(bf16[128,256]{1,0:T(8,128)(2,1)} %param.8) | copy-start | bytes 196612
  193.8 20.3 %all-to-all-start.2 = ((bf16[128,2,256]{2,1,0:T(2,128)(2,1)}), bf16[128,2,256]{2,1,0:T(2,128)(2,1)S(1)}, u32[]{:S(2)}, u32[]{:S(2)}) async-start(bf16[128,2,256]{2,1,0:T(2,128)(2,1)} %all_to_all.27), calls=%async_computation.2 | async-start | bytes 262144 | tf_op jit(solution)/shard_map/all_to_all | solution.py:58
  204.0 174.6 %all-reduce.3.cloned.1.call-start = ((), (), s32[]{:S(2)}) async-start(), calls=%async_computation.3 | async-start | bytes 12582912 | tf_op jit(solution)/shard_map/psum | solution.py:66
Sparse Core Ops, SparseCore 0:
  223.9 154.6 all-reduce.2
where the time goes:
time: 391 us; the launch traced here: 389 us
  waiting for transfers between devices  251 us (64%)
  local copies, waits for them, and re-layouts  51.3 us (13%)
  matrix products  39.8 us (10%)
  starting transfers between devices  32.2 us (8%)
  between operations  14.2 us (4%)
    psum x1, waiting for transfers between devices, on_device(): totals = lax.psum((grad_win, grad_whid, grad_wout), 'dev')  146 us
    all_to_all x1, waiting for transfers between devices, on_device(): lax.all_to_all(send_target, 'dev', split_axis=0, concat_axis=0, tiled=True)  94.9 us
    convert_element_type x1, local copies, waits for them, and re-layouts, on_device(): got_target.astype(jnp.float32)  16.3 us
    dot_general x4, matrix products, inner_rows(): lax.dot_general(left, right, (((0,), (0,)), ((), ())), preferred_element_...  16.2 us
    all_to_all x1, local copies, waits for them, and re-layouts, on_device(): lax.all_to_all(send_target, 'dev', split_axis=0, concat_axis=0, tiled=True)  14.8 us
    scatter x1, local copies, waits for them, and re-layouts, on_device(): jnp.zeros((devices * capacity, vert_width), jnp.bfloat16).at[slot_row]  12 us
    all_to_all x1, starting transfers between devices, on_device(): lax.all_to_all(send_feat, 'dev', split_axis=0, concat_axis=0, tiled=True)  11.5 us
    dot_general x1, matrix products, on_device(): jnp.dot(got_feat, local_basis, preferred_element_type=jnp.float32)  11.1 us
  transfers between devices with their start and end apart: 4, of which 3 were waited for; matrix products, arithmetic and copies ran while one was open for 5% of the time, Pallas kernels for 0%

commit v1 on v0

v1 whole, which is shorter than its diff:
```python
import functools
import jax
import jax.numpy as jnp
from jax import lax
from jax.experimental import pallas as pl
from jax.experimental.pallas import tpu as pltpu
from jax.sharding import PartitionSpec as P

MESH = pl.DeviceIdType.MESH
F32, BF16 = jnp.float32, jnp.bfloat16
CHUNKS, CHUNK, PIECE = 7, 2304, 768
STRIDE = 45
LAST = CHUNKS - 1


def mm(left, right):
    return jnp.dot(left, right, preferred_element_type=F32)


def mm_t(left, right):
    return lax.dot_general(left, right, (((1,), (1,)), ((), ())), preferred_element_type=F32)


def silu_slope(value, sig):
    return sig * (1.0 + value * (1.0 - sig))


def place(me):
    return me // 32, (me // 8) % 4, (me // 2) % 4, me % 2


def device(z, y, x, c):
    return ((z * 4 + y) * 4 + x) * 2 + c


def peer(me, step):
    z, y, x, c = place(me)
    oz, oy, ox, oc = place((step * STRIDE) % 128)
    return device((z + oz) % 4, (y + oy) % 4, (x + ox) % 4, (c + oc) % 2)


def select_matrix(subject, owner):
    n = owner.shape[1]
    down = lax.broadcasted_iota(jnp.int32, (n, n), 0)
    across = lax.broadcasted_iota(jnp.int32, (n, n), 1)
    subject = jnp.broadcast_to(subject.astype(F32), (n, n))
    subject_row = jnp.sum(jnp.where(down == across, subject, 0.0), axis=0, keepdims=True)
    same = subject == subject_row
    rank = jnp.sum(jnp.where(same & (down < across), 1.0, 0.0), axis=0, keepdims=True)
    owner = jnp.broadcast_to(owner.astype(F32), (n, n))
    owner_col = jnp.sum(jnp.where(down == across, owner, 0.0), axis=1, keepdims=True)
    named = subject_row == down.astype(F32)
    slot = jnp.sum(jnp.where(named, owner_col, 0.0), axis=0, keepdims=True)
    row = 2.0 * slot + rank
    rows = lax.broadcasted_iota(jnp.int32, (2 * n, n), 0).astype(F32)
    return jnp.where(rows == row, 1.0, 0.0).astype(BF16)


def kernel(
    pose_h, tgt_h, basis_h, w_in, w_hid, w_out, subject, owner,
    gb_h, gwo, gwh, gwi,
    rows, basis, send, got, stage, pick, feat, feat_t, pose, h1_t, h2_t, slope1_t, slope2, grad_feat,
    parts, sums0, sums1, got0, got1, got2,
    load_sem, stage_sem, send_sem, got_sem, rs_send, rs_got,
):
    me = lax.axis_index("dev")
    z, y, x, c = place(me)
    width = tgt_h.shape[1]
    scale = width ** (-0.5)
    head = pose_h.shape[1]
    first = CHUNK - head

    loads = [
        pltpu.make_async_copy(pose_h, rows.at[:, 0:head], load_sem.at[0]),
        pltpu.make_async_copy(tgt_h.at[:, 0:first], rows.at[:, head:CHUNK], load_sem.at[1]),
        pltpu.make_async_copy(
            tgt_h.at[:, first:width], rows.at[:, CHUNK : head + width], load_sem.at[2]
        ),
        pltpu.make_async_copy(basis_h.at[0], basis.at[:, head : head + width], load_sem.at[3]),
    ]
    for load in loads:
        load.start()

    barrier = pltpu.get_barrier_semaphore()

    def greet(step, carry):
        pl.semaphore_signal(barrier, inc=1, device_id=(peer(me, step),), device_id_type=MESH)
        return carry

    lax.fori_loop(1, 128, greet, 0)

    rows[:, head + width :] = jnp.zeros((rows.shape[0], rows.shape[1] - head - width), BF16)
    basis[:, head + width :] = jnp.zeros((basis.shape[0], basis.shape[1] - head - width), BF16)
    basis[:, 0:head] = jnp.zeros((basis.shape[0], head), BF16)
    pick[...] = select_matrix(subject[...], owner[...])

    def fill(k):
        def piece(j, carry):
            at = pl.multiple_of(k * CHUNK + j * PIECE, 128)
            to = pl.multiple_of(j * PIECE, 128)
            block = mm(pick[...], rows[:, pl.ds(at, PIECE)]).astype(BF16)
            send[k, :, :, pl.ds(to, PIECE)] = block.reshape(128, 2, PIECE)
            return carry

        lax.fori_loop(0, CHUNK // PIECE, piece, 0)

    def ship(k):
        pltpu.make_async_copy(send.at[k, me], got.at[k, me], got_sem.at[k]).start()

        def one(step, carry):
            to = peer(me, step)
            pltpu.make_async_remote_copy(
                src_ref=send.at[k, to],
                dst_ref=got.at[k, me],
                send_sem=send_sem.at[k],
                recv_sem=got_sem.at[k],
                device_id=(to,),
                device_id_type=MESH,
            ).start()
            return carry

        lax.fori_loop(1, 128, one, 0)

    loads[0].wait()
    loads[1].wait()
    fill(0)
    pl.semaphore_wait(barrier, 127)
    ship(0)
    loads[2].wait()

    def more(k, carry):
        fill(k)
        ship(k)
        return carry

    lax.fori_loop(1, CHUNKS, more, 0)
    loads[3].wait()

    def arrived(k):
        pltpu.make_async_copy(got.at[k], got.at[k], got_sem.at[k]).wait()

    arrived(0)
    pose[...] = got[0, :, :, 0:head].reshape(256, head)
    pre_one = mm(pose[...], w_in[...])
    sig_one = jax.nn.sigmoid(pre_one)
    hidden_one = (pre_one * sig_one).astype(BF16)
    h1_t[...] = hidden_one.T
    slope1_t[...] = silu_slope(pre_one, sig_one).T
    pre_two = mm(hidden_one, w_hid[...])
    sig_two = jax.nn.sigmoid(pre_two)
    hidden_two = (pre_two * sig_two).astype(BF16)
    h2_t[...] = hidden_two.T
    slope2[...] = silu_slope(pre_two, sig_two)
    feat[...] = mm(hidden_two, w_out[...]).astype(BF16)
    feat_t[...] = feat[...].T
    grad_feat[...] = jnp.zeros_like(grad_feat)

    def correct(k):
        def piece(j, carry):
            at = pl.multiple_of(k * CHUNK + j * PIECE, 128)
            to = pl.multiple_of(j * PIECE, 128)
            slab = basis[:, pl.ds(at, PIECE)]
            target = got[k, :, :, pl.ds(to, PIECE)].reshape(256, PIECE)
            corr = ((mm(feat[...], slab) - target.astype(F32)) * scale).astype(BF16)
            stage[k % 2, :, pl.ds(to, PIECE)] = corr
            grad_feat[...] += mm_t(corr, slab)
            return carry

        lax.fori_loop(0, CHUNK // PIECE, piece, 0)

    def outer(k):
        def piece(j, carry):
            to = pl.multiple_of(j * PIECE, 128)
            corr = stage[k % 2, :, pl.ds(to, PIECE)]
            stage[k % 2, :, pl.ds(to, PIECE)] = mm(feat_t[...], corr).astype(BF16)
            return carry

        lax.fori_loop(0, CHUNK // PIECE, piece, 0)

    def store(k):
        if isinstance(k, int) and k == 0:
            return pltpu.make_async_copy(
                stage.at[0, :, head:CHUNK], gb_h.at[0, :, 0:first], stage_sem.at[0]
            )
        if isinstance(k, int) and k == LAST:
            size = width - (LAST * CHUNK - head)
            return pltpu.make_async_copy(
                stage.at[k % 2, :, 0:size],
                gb_h.at[0, :, LAST * CHUNK - head : width],
                stage_sem.at[k % 2],
            )
        at = pl.multiple_of(k * CHUNK - head, 128)
        return pltpu.make_async_copy(
            stage.at[k % 2], gb_h.at[0, :, pl.ds(at, CHUNK)], stage_sem.at[k % 2]
        )

    correct(0)
    outer(0)
    store(0).start()
    arrived(1)
    correct(1)
    outer(1)
    store(1).start()
    store(0).wait()

    def middle(k, carry):
        arrived(k)
        correct(k)
        outer(k)
        store(k).start()
        store(k - 1).wait()
        return carry

    lax.fori_loop(2, LAST, middle, 0)
    arrived(LAST)
    correct(LAST)

    grad = grad_feat[...].astype(BF16)
    back_two = (mm_t(grad, w_out[...]) * slope2[...]).astype(BF16)
    back_one_t = (mm_t(w_hid[...], back_two) * slope1_t[...]).astype(BF16)
    for third in range(3):
        if third == 0:
            upper = mm(h2_t[...], grad)
        else:
            upper = mm(h1_t[...], back_two[:, 256 * (third - 1) : 256 * third])
        if third == 2:
            lower = mm(back_one_t, pose[...])
        else:
            lower = mm(h1_t[...], back_two[:, 512 + 256 * third : 768 + 256 * third])
        both = jnp.concatenate([upper.reshape(128, 8, 256), lower.reshape(128, 8, 256)], axis=1)
        parts[third] = both.astype(BF16).reshape(64, 2, 16, 256)

    twin = device(z, y, x, 1 - c)
    copies0 = []
    for third in range(3):
        copies0.append(
            pltpu.make_async_remote_copy(
                src_ref=parts.at[third, :, 1 - c],
                dst_ref=got0.at[third],
                send_sem=rs_send.at[0, third],
                recv_sem=rs_got.at[0, third],
                device_id=(twin,),
                device_id_type=MESH,
            )
        )
        copies0[-1].start()
    outer(LAST)
    store(LAST).start()
    store(LAST - 1).wait()

    spots = (x, y, z)

    def along(third, value):
        zyx = [z, y, x]
        zyx[2 - third] = value
        return device(*zyx, c)

    def rows1(ref, third, value):
        view = ref.at[third]
        if third == 0:
            return view.at[:, :, value]
        if third == 1:
            return view.at[:, value]
        return view.at[value]

    copies1 = []
    for third in range(3):
        copies0[third].wait_recv()
        own = parts[third, :, c].astype(F32)
        sums0[third] = (own + got0[third].astype(F32)).astype(BF16).reshape(4, 4, 4, 16, 256)
        for hop in (1, 3, 2):
            value = (spots[third] + hop) % 4
            copy = pltpu.make_async_remote_copy(
                src_ref=rows1(sums0, third, value),
                dst_ref=got1.at[third, hop - 1],
                send_sem=rs_send.at[hop, third],
                recv_sem=rs_got.at[hop, third],
                device_id=(along(third, value),),
                device_id_type=MESH,
            )
            copy.start()
            copies1.append((third, copy))

    def plane(third, a, b):
        if third == 0:
            return device(a, b, x, c)
        if third == 1:
            return device(a, y, b, c)
        return device(z, a, b, c)

    mine = ((z, y), (z, x), (y, x))
    for third in range(3):
        for which, copy in copies1:
            if which == third:
                copy.wait_recv()
        if third == 0:
            own = sums0[third, :, :, x]
        elif third == 1:
            own = sums0[third, :, y]
        else:
            own = sums0[third, z]
        total = own.astype(F32)
        for hop in range(3):
            total = total + got1[third, hop].astype(F32)
        sums1[third] = total.astype(BF16)
        a0, b0 = mine[third]

        def one(step, carry, third=third, a0=a0, b0=b0):
            off = (step * 5) % 16
            a, b = (a0 + off // 4) % 4, (b0 + off % 4) % 4
            pltpu.make_async_remote_copy(
                src_ref=sums1.at[third, a, b],
                dst_ref=got2.at[third, off - 1],
                send_sem=rs_send.at[4, third],
                recv_sem=rs_got.at[4, third],
                device_id=(plane(third, a, b),),
                device_id_type=MESH,
            ).start()
            return carry

        lax.fori_loop(1, 16, one, 0)

    for third in range(3):
        pltpu.make_async_copy(got2.at[third], got2.at[third], rs_got.at[4, third]).wait()
        a0, b0 = mine[third]
        total = sums1[third, a0, b0].astype(F32)
        total = total + jnp.sum(got2[third].astype(F32), axis=0)
        upper, lower = total[0:8], total[8:16]
        if third == 0:
            gwo[...] = upper
        else:
            gwh[:, 256 * (third - 1) : 256 * third] = upper
        if third == 2:
            gwi[...] = lower
        else:
            gwh[:, 512 + 256 * third : 768 + 256 * third] = lower

    def sent(k, carry):
        sample = send.at[k, pl.ds(0, 127)]
        pltpu.make_async_copy(sample, sample, send_sem.at[k]).wait()
        return carry

    lax.fori_loop(0, CHUNKS, sent, 0)
    for copy in copies0:
        copy.wait_send()
    for _, copy in copies1:
        copy.wait_send()
    for third in range(3):
        pltpu.make_async_copy(got2.at[third], got2.at[third], rs_send.at[4, third]).wait()
    store(LAST).wait()


def on_device(pose_input, w_in, w_hid, w_out, targets, basis, owner, frame_subject):
    frames, p_size = pose_input.shape
    width = targets.shape[1]
    hidden = w_hid.shape[0]
    vmem = pl.BlockSpec(memory_space=pltpu.VMEM)
    hbm = pl.BlockSpec(memory_space=pl.ANY)
    padded = CHUNKS * CHUNK
    grad_basis, gwo, gwh, gwi = pl.pallas_call(
        kernel,
        out_shape=(
            jax.ShapeDtypeStruct(basis.shape, BF16),
            jax.ShapeDtypeStruct((8, p_size), F32),
            jax.ShapeDtypeStruct((8, hidden), F32),
            jax.ShapeDtypeStruct((8, p_size), F32),
        ),
        in_specs=[hbm, hbm, hbm, vmem, vmem, vmem, vmem, vmem],
        out_specs=(hbm, vmem, vmem, vmem),
        scratch_shapes=[
            pltpu.VMEM((frames, padded), BF16),
            pltpu.VMEM((p_size, padded), BF16),
            pltpu.VMEM((CHUNKS, 128, 2, CHUNK), BF16),
            pltpu.VMEM((CHUNKS, 128, 2, CHUNK), BF16),
            pltpu.VMEM((2, p_size, CHUNK), BF16),
            pltpu.VMEM((256, frames), BF16),
            pltpu.VMEM((256, p_size), BF16),
            pltpu.VMEM((p_size, 256), BF16),
            pltpu.VMEM((256, p_size), BF16),
            pltpu.VMEM((hidden, 256), BF16),
            pltpu.VMEM((hidden, 256), BF16),
            pltpu.VMEM((hidden, 256), F32),
            pltpu.VMEM((256, hidden), F32),
            pltpu.VMEM((256, p_size), F32),
            pltpu.VMEM((3, 64, 2, 16, 256), BF16),
            pltpu.VMEM((3, 4, 4, 4, 16, 256), BF16),
            pltpu.VMEM((3, 4, 4, 16, 256), BF16),
            pltpu.VMEM((3, 64, 16, 256), BF16),
            pltpu.VMEM((3, 3, 4, 4, 16, 256), BF16),
            pltpu.VMEM((3, 15, 16, 256), BF16),
            pltpu.SemaphoreType.DMA((4,)),
            pltpu.SemaphoreType.DMA((2,)),
            pltpu.SemaphoreType.DMA((CHUNKS,)),
            pltpu.SemaphoreType.DMA((CHUNKS,)),
            pltpu.SemaphoreType.DMA((5, 3)),
            pltpu.SemaphoreType.DMA((5, 3)),
        ],
        compiler_params=pltpu.CompilerParams(
            collective_id=0, has_side_effects=True, vmem_limit_bytes=60 * 2**20
        ),
    )(
        pose_input, targets, basis, w_in, w_hid, w_out,
        frame_subject.astype(jnp.int32), owner.astype(jnp.int32).reshape(1, -1),
    )
    return gwi.T, gwh, gwo, grad_basis


def solution(mesh):
    in_specs = (
        P("dev", None),
        P(),
        P(),
        P(),
        P("dev", None),
        P("dev", None, None),
        P(),
        P("dev", None),
    )
    out_specs = (P(None, "dev"), P("dev", None), P("dev", None), P("dev", None, None))
    return jax.shard_map(
        on_device, mesh=mesh, in_specs=in_specs, out_specs=out_specs, check_vma=False
    )
```

time: 391 us -> 143 us (0.37)
  waiting for transfers between devices: 251 us -> 0 us
  Pallas kernels: 0 us -> 129 us
  matrix products: 39.8 us -> 0 us
  local copies, waits for them, and re-layouts: 51.3 us -> 12.5 us
  starting transfers between devices: 32.2 us -> 0 us
  between operations: 14.2 us -> 0.64 us
    psum x1 -> x0, waiting for transfers between devices: 146 us -> none  [on_device(): totals = lax.psum((grad_win, grad_whid, grad_wout), 'dev')]
    pallas_call x0 -> x1, Pallas kernels: none -> 129 us  [on_device(): pl.pallas_call(kernel, out_shape=(jax.ShapeDtypeStruct(basis.shape, BF16)...]
    all_to_all x3 -> x0, waiting for transfers between devices: 105 us -> none  [the longest x1 94.9 us: on_device(): lax.all_to_all(send_target, 'dev', split_axis=0, concat_axis=0, tiled=True)]
    dot_general x10 -> x0, matrix products: 39.8 us -> none  [the longest x4 16.2 us: inner_rows(): lax.dot_general(left, right, (((0,), (0,)), ((), ())), preferred_element_...]
    all_to_all x3 -> x0, starting transfers between devices: 31.9 us -> none  [the longest x1 11.5 us: on_device(): lax.all_to_all(send_feat, 'dev', split_axis=0, concat_axis=0, tiled=True)]
    convert_element_type x1 -> x0, local copies, waits for them, and re-layouts: 16.3 us -> none  [on_device(): got_target.astype(jnp.float32)]
    all_to_all x5 -> x0, local copies, waits for them, and re-layouts: 16.3 us -> none  [the longest x1 14.8 us: on_device(): lax.all_to_all(send_target, 'dev', split_axis=0, concat_axis=0, tiled=True)]
    scatter x2 -> x0, local copies, waits for them, and re-layouts: 13.1 us -> none  [the longest x1 12 us: on_device(): jnp.zeros((devices * capacity, vert_width), jnp.bfloat16).at[slot_row]]
  transfers between devices with their start and end apart: 4 -> 0, of which waited for: 3 -> 0; matrix products, arithmetic and copies ran while one was open for 5% -> 0% of each run, Pallas kernels for 0% -> 0%
where the time goes in v1:
time: 143 us; the launch traced here: 142 us
  Pallas kernels  129 us (90%)
  local copies, waits for them, and re-layouts  12.5 us (9%)
    pallas_call x1, Pallas kernels, on_device(): pl.pallas_call(kernel, out_shape=(jax.ShapeDtypeStruct(basis.shape, BF16)...  129 us
    unnamed x5, local copies, waits for them, and re-layouts  12.5 us

profile of v1, /device:TPU:1, one launch (start us, length us, event | category | flops | bytes accessed | tf_op | source)
XLA Modules:
  0.0 142.4 jit_solution(13750414583817492820)
XLA Ops:
  0.6 1.4 copy.12.subject
  2.0 129.3 %shard_map.111 = (bf16[1,256,15744]{2,1,0:T(8,128)(2,1)}, f32[8,256]{1,0:T(8,128)}, f32[8,1024]{1,0:T(8,128)}, f32[8,256]{1,0:T(8,128)}) custom-call(bf16[128,256]{1,0:T(8,128)(2,1)} %pose_h.1, bf16[128,15744]{1,0:T(8,128)(2,1)} %tgt_h.1, bf16[1,256,15744]{2,1,0:T(8,128)(2,1)} %basis_h.1, bf16[256,1024]{1,0:T(8,128)(2,1)} %w_in.1, bf16[1024,1024]{1,0:T(8,128)(2,1)} %w_hid.1, ...), custom_call_target="tpu_custom_call" | custom-call | tf_op jit(solution)/shard_map/pallas_call | solution.py:360
  131.3 1.3 copy.17
  132.6 1.4 copy.18
  134.0 1.3 copy.19
  135.3 7.1 %copy.20 = bf16[1,256,15744]{2,1,0:T(8,128)(2,1)} copy(bf16[1,256,15744]{2,1,0:T(8,128)(2,1)} %get-tuple-element.19) | data formatting | bytes 16121856

commit v2 on v1

v2 whole, which is shorter than its diff:
```python
import functools
import jax
import jax.numpy as jnp
from jax import lax
from jax.experimental import pallas as pl
from jax.experimental.pallas import tpu as pltpu
from jax.sharding import PartitionSpec as P

MESH = pl.DeviceIdType.MESH
F32, BF16 = jnp.float32, jnp.bfloat16
CHUNKS, CHUNK, PIECE = 7, 2304, 768
STRIDE = 37
LAST = CHUNKS - 1
VMEM_LIMIT = 54 * 2**20


def mm(left, right):
    return jnp.dot(left, right, preferred_element_type=F32)


def mm_t(left, right):
    return lax.dot_general(left, right, (((1,), (1,)), ((), ())), preferred_element_type=F32)


def silu_slope(value, sig):
    return sig * (1.0 + value * (1.0 - sig))


def device(z, y, x, c):
    return ((z * 4 + y) * 4 + x) * 2 + c


def peer(me, step):
    return lax.rem(me + step * STRIDE, 128)


def select_matrix(subject, owner):
    n = owner.shape[1]
    down = lax.broadcasted_iota(jnp.int32, (n, n), 0)
    across = lax.broadcasted_iota(jnp.int32, (n, n), 1)
    subject_row = subject.astype(F32)
    wide = jnp.broadcast_to(subject_row, (n, n))
    subject_col = jnp.sum(jnp.where(down == across, wide, 0.0), axis=1, keepdims=True)
    same = subject_col == subject_row
    rank = jnp.sum(jnp.where(same & (down < across), 1.0, 0.0), axis=0, keepdims=True)
    owner = jnp.broadcast_to(owner.astype(F32), (n, n))
    owner_col = jnp.sum(jnp.where(down == across, owner, 0.0), axis=1, keepdims=True)
    named = subject_row == down.astype(F32)
    slot = jnp.sum(jnp.where(named, owner_col, 0.0), axis=0, keepdims=True)
    row = 2.0 * slot + rank
    rows = lax.broadcasted_iota(jnp.int32, (2 * n, n), 0).astype(F32)
    return jnp.where(rows == row, 1.0, 0.0).astype(BF16)


def half_matrix(c, rows, columns):
    row = lax.broadcasted_iota(jnp.int32, (rows, columns), 0)
    column = lax.broadcasted_iota(jnp.int32, (rows, columns), 1)
    return jnp.where(column == 2 * row - row % 8 + 8 * c, 1.0, 0.0).astype(BF16)


def kernel(
    pose_h, tgt_h, basis_h, w_in, w_hid, w_out, subject, owner,
    gb, gwo, gwh, gwi,
    rows, basis, send, got, pick, feat, feat_t, pose, half, w_in_t, w_hid_half,
    h1_t, h2_t, slope1_t, slope2, grad_feat, grad, back_two, back_one_t,
    sums0, sums1, got1, got2,
    load_sem, send_sem, got_sem, rs_send, rs_got,
):
    me = lax.axis_index("dev")
    z, y, x, c = me // 32, (me // 8) % 4, (me // 2) % 4, me % 2
    width = tgt_h.shape[1]
    scale = width ** (-0.5)
    head = pose_h.shape[1]
    first = CHUNK - head
    rest = head + width - LAST * CHUNK

    loads = [
        pltpu.make_async_copy(pose_h, rows.at[:, 0:head], load_sem.at[0]),
        pltpu.make_async_copy(tgt_h.at[:, 0:first], rows.at[:, head:CHUNK], load_sem.at[1]),
        pltpu.make_async_copy(
            tgt_h.at[:, first:width], rows.at[:, CHUNK : head + width], load_sem.at[2]
        ),
        pltpu.make_async_copy(basis_h.at[0], basis.at[:, head : head + width], load_sem.at[3]),
    ]
    for load in loads:
        load.start()

    barrier = pltpu.get_barrier_semaphore()

    def greet(step, carry):
        pl.semaphore_signal(barrier, inc=1, device_id=(peer(me, step),), device_id_type=MESH)
        return carry

    lax.fori_loop(1, 128, greet, 0)

    rows[:, head + width :] = jnp.zeros((rows.shape[0], rows.shape[1] - head - width), BF16)
    basis[:, head + width :] = jnp.zeros((basis.shape[0], basis.shape[1] - head - width), BF16)
    basis[:, 0:head] = jnp.zeros((basis.shape[0], head), BF16)
    got[LAST, :, :, rest:] = jnp.zeros((128, 2, CHUNK - rest), BF16)
    pick[...] = select_matrix(subject[...], owner[...])

    def fill(k):
        def piece(j, carry):
            at = pl.multiple_of(k * CHUNK + j * PIECE, 128)
            to = pl.multiple_of(j * PIECE, 128)
            block = mm(pick[...], rows[:, pl.ds(at, PIECE)]).astype(BF16)
            send[k, :, :, pl.ds(to, PIECE)] = block.reshape(128, 2, PIECE)
            return carry

        lax.fori_loop(0, CHUNK // PIECE, piece, 0)

    def ship(k, size):
        pltpu.make_async_copy(
            send.at[k, me, :, 0:size], got.at[k, me, :, 0:size], got_sem.at[k]
        ).start()

        def one(step, carry):
            to = peer(me, step)
            pltpu.make_async_remote_copy(
                src_ref=send.at[k, to, :, 0:size],
                dst_ref=got.at[k, me, :, 0:size],
                send_sem=send_sem.at[k],
                recv_sem=got_sem.at[k],
                device_id=(to,),
                device_id_type=MESH,
            ).start()
            return carry

        lax.fori_loop(1, 128, one, 0)

    loads[0].wait()
    loads[1].wait()
    fill(0)
    pl.semaphore_wait(barrier, 127)
    ship(0, CHUNK)
    loads[2].wait()

    def more(k, carry):
        fill(k)
        ship(k, CHUNK)
        return carry

    lax.fori_loop(1, LAST, more, 0)
    fill(LAST)
    ship(LAST, rest)

    half[...] = half_matrix(c, half.shape[0], half.shape[1])
    w_in_t[...] = mm_t(half[...], w_in[...]).astype(BF16)
    w_hid_half[...] = mm(half[...], w_hid[...]).astype(BF16)
    loads[3].wait()

    def arrived(k, size):
        block = got.at[k, :, :, 0:size]
        pltpu.make_async_copy(block, block, got_sem.at[k]).wait()

    def forward(part):
        at = 256 * part
        pre_one = mm(pose[at : at + 256, :], w_in[...])
        hidden_one = (pre_one * jax.nn.sigmoid(pre_one)).astype(BF16)
        pre_two = mm(hidden_one, w_hid[...])
        sig_two = jax.nn.sigmoid(pre_two)
        hidden_two = (pre_two * sig_two).astype(BF16)
        slope2[at : at + 256, :] = silu_slope(pre_two, sig_two)
        h2_t[:, at : at + 256] = mm_t(half[...], hidden_two).astype(BF16)
        return hidden_two

    twin = device(z, y, x, 1 - c)

    def to_twin(ref, slot):
        return pltpu.make_async_remote_copy(
            src_ref=ref.at[0:256],
            dst_ref=ref.at[256:512],
            send_sem=rs_send.at[0, slot],
            recv_sem=rs_got.at[0, slot],
            device_id=(twin,),
            device_id_type=MESH,
        )

    arrived(0, CHUNK)
    pose[0:256, :] = got[0, :, :, 0:head].reshape(256, head)
    pose_copy = to_twin(pose, 0)
    pose_copy.start()
    feat[...] = mm(forward(0), w_out[...]).astype(BF16)
    feat_t[...] = feat[...].T
    grad_feat[...] = jnp.zeros_like(grad_feat)

    def correct(k):
        def piece(j, carry):
            at = pl.multiple_of(k * CHUNK + j * PIECE, 128)
            to = pl.multiple_of(j * PIECE, 128)
            slab = basis[:, pl.ds(at, PIECE)]
            target = got[k, :, :, pl.ds(to, PIECE)].reshape(256, PIECE)
            corr = ((mm(feat[...], slab) - target.astype(F32)) * scale).astype(BF16)
            gb[:, pl.ds(at, PIECE)] = corr
            grad_feat[...] += mm_t(corr, slab)
            return carry

        lax.fori_loop(0, CHUNK // PIECE, piece, 0)

    def outer(k):
        def piece(j, carry):
            at = pl.multiple_of(k * CHUNK + j * PIECE, 128)
            gb[:, pl.ds(at, PIECE)] = mm(feat_t[...], gb[:, pl.ds(at, PIECE)]).astype(BF16)
            return carry

        lax.fori_loop(0, CHUNK // PIECE, piece, 0)

    def turn(k, carry):
        arrived(k, CHUNK)
        correct(k)
        outer(k)
        return carry

    correct(0)
    outer(0)
    lax.fori_loop(1, 3, turn, 0)
    pose_copy.wait_recv()
    forward(1)
    pre_t = mm_t(w_in_t[...], pose[...])
    sig_t = jax.nn.sigmoid(pre_t)
    h1_t[...] = (pre_t * sig_t).astype(BF16)
    slope1_t[...] = silu_slope(pre_t, sig_t)
    lax.fori_loop(3, LAST, turn, 0)
    arrived(LAST, rest)
    correct(LAST)

    grad[0:256, :] = grad_feat[...].astype(BF16)
    grad_copy = to_twin(grad, 1)
    grad_copy.start()

    def backward(part):
        at = 256 * part
        back = mm_t(grad[at : at + 256, :], w_out[...]) * slope2[at : at + 256, :]
        back_two[at : at + 256, :] = back.astype(BF16)

    backward(0)
    grad_copy.wait_recv()
    backward(1)

    spots = (x, y, z)

    def along(third, value):
        zyx = [z, y, x]
        zyx[2 - third] = value
        return device(*zyx, c)

    def rows1(ref, third, value):
        view = ref.at[third]
        if third == 0:
            return view.at[:, :, value]
        if third == 1:
            return view.at[:, value]
        return view.at[value]

    copies1 = []
    for third in range(3):
        if third == 0:
            upper = mm(h2_t[...], grad[...])
        else:
            upper = mm(h1_t[...], back_two[:, 256 * (third - 1) : 256 * third])
        if third == 2:
            back = mm_t(w_hid_half[...], back_two[...]) * slope1_t[...]
            back_one_t[...] = back.astype(BF16)
            lower = mm(back_one_t[...], pose[...])
        else:
            lower = mm(h1_t[...], back_two[:, 512 + 256 * third : 768 + 256 * third])
        both = jnp.concatenate([upper.reshape(64, 8, 256), lower.reshape(64, 8, 256)], axis=1)
        sums0[third] = both.astype(BF16).reshape(4, 4, 4, 16, 256)
        for hop in (1, 3, 2):
            value = (spots[third] + hop) % 4
            copy = pltpu.make_async_remote_copy(
                src_ref=rows1(sums0, third, value),
                dst_ref=got1.at[third, hop - 1],
                send_sem=rs_send.at[hop, third],
                recv_sem=rs_got.at[hop, third],
                device_id=(along(third, value),),
                device_id_type=MESH,
            )
            copy.start()
            copies1.append((third, copy))
    outer(LAST)

    def plane(third, a, b):
        if third == 0:
            return device(a, b, x, c)
        if third == 1:
            return device(a, y, b, c)
        return device(z, a, b, c)

    mine = ((z, y), (z, x), (y, x))
    for third in range(3):
        for which, copy in copies1:
            if which == third:
                copy.wait_recv()
        if third == 0:
            own = sums0[third, :, :, x]
        elif third == 1:
            own = sums0[third, :, y]
        else:
            own = sums0[third, z]
        total = own.astype(F32)
        for hop in range(3):
            total = total + got1[third, hop].astype(F32)
        sums1[third] = total.astype(BF16)
        a0, b0 = mine[third]
        for off in (5, 15, 4, 1, 12, 3, 13, 7, 10, 8, 2, 6, 9, 14, 11):
            a, b = (a0 + off // 4) % 4, (b0 + off % 4) % 4
            pltpu.make_async_remote_copy(
                src_ref=sums1.at[third, a, b],
                dst_ref=got2.at[third, off - 1],
                send_sem=rs_send.at[4, third],
                recv_sem=rs_got.at[4, third],
                device_id=(plane(third, a, b),),
                device_id_type=MESH,
            ).start()

    for third in range(3):
        pltpu.make_async_copy(got2.at[third], got2.at[third], rs_got.at[4, third]).wait()
        a0, b0 = mine[third]
        total = sums1[third, a0, b0].astype(F32)
        total = total + jnp.sum(got2[third].astype(F32), axis=0)
        upper, lower = total[0:8], total[8:16]
        if third == 0:
            gwo[...] = upper
        else:
            gwh[:, 256 * (third - 1) : 256 * third] = upper
        if third == 2:
            gwi[...] = lower
        else:
            gwh[:, 512 + 256 * third : 768 + 256 * third] = lower

    def sent(k, size):
        sample = send.at[k, pl.ds(0, 127), :, 0:size]
        pltpu.make_async_copy(sample, sample, send_sem.at[k]).wait()

    def all_sent(k, carry):
        sent(k, CHUNK)
        return carry

    lax.fori_loop(0, LAST, all_sent, 0)
    sent(LAST, rest)
    pose_copy.wait_send()
    grad_copy.wait_send()
    for _, copy in copies1:
        copy.wait_send()
    for third in range(3):
        pltpu.make_async_copy(got2.at[third], got2.at[third], rs_send.at[4, third]).wait()


def deliver(head, gb, gwo, gwh, gwi, gb_h, gwo_h, gwh_h, gwi_h, sem):
    width = gb_h.shape[2]
    copies = [
        pltpu.make_async_copy(gb.at[:, head : head + width], gb_h.at[0], sem.at[0]),
        pltpu.make_async_copy(gwo, gwo_h, sem.at[1]),
        pltpu.make_async_copy(gwh, gwh_h, sem.at[2]),
        pltpu.make_async_copy(gwi, gwi_h, sem.at[3]),
    ]
    for copy in copies:
        copy.start()
    for copy in copies:
        copy.wait()


def on_device(pose_input, w_in, w_hid, w_out, targets, basis, owner, frame_subject):
    frames, p_size = pose_input.shape
    hidden = w_hid.shape[0]
    vmem = pl.BlockSpec(memory_space=pltpu.VMEM)
    hbm = pl.BlockSpec(memory_space=pl.ANY)
    padded = CHUNKS * CHUNK
    kept = pl.pallas_call(
        kernel,
        out_shape=(
            pltpu.VMEM((p_size, padded), BF16),
            pltpu.VMEM((8, p_size), F32),
            pltpu.VMEM((8, hidden), F32),
            pltpu.VMEM((8, p_size), F32),
        ),
        in_specs=[hbm, hbm, hbm, vmem, vmem, vmem, vmem, vmem],
        out_specs=(vmem, vmem, vmem, vmem),
        scratch_shapes=[
            pltpu.VMEM((frames, padded), BF16),
            pltpu.VMEM((p_size, padded), BF16),
            pltpu.VMEM((CHUNKS, 128, 2, CHUNK), BF16),
            pltpu.VMEM((CHUNKS, 128, 2, CHUNK), BF16),
            pltpu.VMEM((256, frames), BF16),
            pltpu.VMEM((256, p_size), BF16),
            pltpu.VMEM((p_size, 256), BF16),
            pltpu.VMEM((512, p_size), BF16),
            pltpu.VMEM((hidden // 2, hidden), BF16),
            pltpu.VMEM((hidden // 2, p_size), BF16),
            pltpu.VMEM((hidden // 2, hidden), BF16),
            pltpu.VMEM((hidden // 2, 512), BF16),
            pltpu.VMEM((hidden // 2, 512), BF16),
            pltpu.VMEM((hidden // 2, 512), F32),
            pltpu.VMEM((512, hidden), F32),
            pltpu.VMEM((256, p_size), F32),
            pltpu.VMEM((512, p_size), BF16),
            pltpu.VMEM((512, hidden), BF16),
            pltpu.VMEM((hidden // 2, 512), BF16),
            pltpu.VMEM((3, 4, 4, 4, 16, 256), BF16),
            pltpu.VMEM((3, 4, 4, 16, 256), BF16),
            pltpu.VMEM((3, 3, 4, 4, 16, 256), BF16),
            pltpu.VMEM((3, 15, 16, 256), BF16),
            pltpu.SemaphoreType.DMA((4,)),
            pltpu.SemaphoreType.DMA((CHUNKS,)),
            pltpu.SemaphoreType.DMA((CHUNKS,)),
            pltpu.SemaphoreType.DMA((5, 3)),
            pltpu.SemaphoreType.DMA((5, 3)),
        ],
        compiler_params=pltpu.CompilerParams(
            collective_id=0, has_side_effects=True, vmem_limit_bytes=VMEM_LIMIT
        ),
    )(
        pose_input, targets, basis, w_in, w_hid, w_out,
        frame_subject.astype(jnp.int32).reshape(1, -1), owner.astype(jnp.int32).reshape(1, -1),
    )
    grad_basis, gwo, gwh, gwi = pl.pallas_call(
        functools.partial(deliver, p_size),
        out_shape=(
            jax.ShapeDtypeStruct(basis.shape, BF16),
            jax.ShapeDtypeStruct((8, p_size), F32),
            jax.ShapeDtypeStruct((8, hidden), F32),
            jax.ShapeDtypeStruct((8, p_size), F32),
        ),
        in_specs=[hbm] * 4,
        out_specs=(hbm,) * 4,
        scratch_shapes=[pltpu.SemaphoreType.DMA((4,))],
        compiler_params=pltpu.CompilerParams(vmem_limit_bytes=2**20),
    )(*(pltpu.with_memory_space_constraint(value, pltpu.VMEM) for value in kept))
    return gwi.T, gwh, gwo, grad_basis


def solution(mesh):
    in_specs = (
        P("dev", None),
        P(),
        P(),
        P(),
        P("dev", None),
        P("dev", None, None),
        P(),
        P("dev", None),
    )
    out_specs = (P(None, "dev"), P("dev", None), P("dev", None), P("dev", None, None))
    return jax.shard_map(
        on_device, mesh=mesh, in_specs=in_specs, out_specs=out_specs, check_vma=False
    )
```

time: 143 us -> 128 us (0.90)
  local copies, waits for them, and re-layouts: 12.5 us -> 0 us
  Pallas kernels: 129 us -> 127 us
    unnamed x5 -> x0, local copies, waits for them, and re-layouts: 12.5 us -> none
    pallas_call x1 -> x2, Pallas kernels: 129 us -> 127 us  [the longest x1 124 us: on_device(): pl.pallas_call(kernel, out_shape=(pltpu.VMEM((p_size, padded), BF16), plt...]
where the time goes in v2:
time: 128 us; the launch traced here: 127 us
  Pallas kernels  127 us (99%)
    pallas_call x1, Pallas kernels, on_device(): pl.pallas_call(kernel, out_shape=(pltpu.VMEM((p_size, padded), BF16), plt...  124 us
    pallas_call x1, Pallas kernels, on_device(): pl.pallas_call(functools.partial(deliver, p_size), out_shape=(jax.ShapeDt...  3.33 us

profile of v2, /device:TPU:1, one launch (start us, length us, event | category | flops | bytes accessed | tf_op | source)
XLA Modules:
  0.0 127.5 jit_solution(4795642750529276070)
XLA Ops:
  0.6 123.5 %shard_map.111 = (bf16[256,16128]{1,0:T(8,128)(2,1)S(1)}, f32[8,256]{1,0:T(8,128)S(1)}, f32[8,1024]{1,0:T(8,128)S(1)}, f32[8,256]{1,0:T(8,128)S(1)}) custom-call(bf16[128,256]{1,0:T(8,128)(2,1)} %pose_h.1, bf16[128,15744]{1,0:T(8,128)(2,1)} %tgt_h.1, bf16[1,256,15744]{2,1,0:T(8,128)(2,1)} %basis_h.1, bf16[256,1024]{1,0:T(8,128)(2,1)} %w_in.1, ...), custom_call_target="tpu_custom_call" | custom-call | tf_op jit(solution)/shard_map/pallas_call | solution.py:370
  124.2 3.3 %shard_map.112 = (bf16[1,256,15744]{2,1,0:T(8,128)(2,1)}, f32[8,256]{1,0:T(8,128)}, f32[8,1024]{1,0:T(8,128)}, f32[8,256]{1,0:T(8,128)}) custom-call(bf16[256,16128]{1,0:T(8,128)(2,1)S(1)} %get-tuple-element.12.gb, f32[8,256]{1,0:T(8,128)S(1)} %get-tuple-element.13.gwo, f32[8,1024]{1,0:T(8,128)S(1)} %get-tuple-element.14.gwh, f32[8,256]{1,0:T(8,128)S(1)} %get-tuple-element.15.gwi), custom_call_target="tpu_custom_call" | custom-call | tf_op jit(solution)/shard_map/pallas_call | solution.py:417

commit v3 on v2

--- a/solution.py
+++ b/solution.py
@@ -12,6 +12,7 @@
 STRIDE = 37
 LAST = CHUNKS - 1
 VMEM_LIMIT = 54 * 2**20
+BLOCKS = 4
 
 
 def mm(left, right):
@@ -59,11 +60,11 @@
 
 
 def kernel(
-    pose_h, tgt_h, basis_h, w_in, w_hid, w_out, subject, owner,
+    pose_h, tgt_h, basis_h, w_in_h, w_hid_h, w_out_h, subject_h, owner_h,
     gb, gwo, gwh, gwi,
-    rows, basis, send, got, pick, feat, feat_t, pose, half, w_in_t, w_hid_half,
+    w_in, w_hid, w_out, subject, owner, rows, basis, send, got, pick, feat, feat_t, pose, half, w_in_t, w_hid_half,
     h1_t, h2_t, slope1_t, slope2, grad_feat, grad, back_two, back_one_t,
-    sums0, sums1, got1, got2,
+    halves, sums0, sums1, got1, got2,
     load_sem, send_sem, got_sem, rs_send, rs_got,
 ):
     me = lax.axis_index("dev")
@@ -74,15 +75,21 @@
     first = CHUNK - head
     rest = head + width - LAST * CHUNK
 
+    pairs = [
+        (subject_h, subject),
+        (owner_h, owner),
+        (pose_h, rows.at[:, 0:head]),
+        (tgt_h.at[:, 0:first], rows.at[:, head:CHUNK]),
+        (tgt_h.at[:, first:width], rows.at[:, CHUNK : head + width]),
+        (w_in_h, w_in),
+        (w_hid_h, w_hid),
+        (w_out_h, w_out),
+        (basis_h.at[0], basis.at[:, head : head + width]),
+    ]
     loads = [
-        pltpu.make_async_copy(pose_h, rows.at[:, 0:head], load_sem.at[0]),
-        pltpu.make_async_copy(tgt_h.at[:, 0:first], rows.at[:, head:CHUNK], load_sem.at[1]),
-        pltpu.make_async_copy(
-            tgt_h.at[:, first:width], rows.at[:, CHUNK : head + width], load_sem.at[2]
-        ),
-        pltpu.make_async_copy(basis_h.at[0], basis.at[:, head : head + width], load_sem.at[3]),
+        pltpu.make_async_copy(src, dst, load_sem.at[at]) for at, (src, dst) in enumerate(pairs)
     ]
-    for load in loads:
+    for load in loads[:4]:
         load.start()
 
     barrier = pltpu.get_barrier_semaphore()
@@ -92,11 +99,15 @@
         return carry
 
     lax.fori_loop(1, 128, greet, 0)
+    for load in loads[4:]:
+        load.start()
 
     rows[:, head + width :] = jnp.zeros((rows.shape[0], rows.shape[1] - head - width), BF16)
     basis[:, head + width :] = jnp.zeros((basis.shape[0], basis.shape[1] - head - width), BF16)
     basis[:, 0:head] = jnp.zeros((basis.shape[0], head), BF16)
     got[LAST, :, :, rest:] = jnp.zeros((128, 2, CHUNK - rest), BF16)
+    loads[0].wait()
+    loads[1].wait()
     pick[...] = select_matrix(subject[...], owner[...])
 
     def fill(k):
@@ -128,12 +139,12 @@
 
         lax.fori_loop(1, 128, one, 0)
 
-    loads[0].wait()
-    loads[1].wait()
+    loads[2].wait()
+    loads[3].wait()
     fill(0)
     pl.semaphore_wait(barrier, 127)
     ship(0, CHUNK)
-    loads[2].wait()
+    loads[4].wait()
 
     def more(k, carry):
         fill(k)
@@ -144,10 +155,11 @@
     fill(LAST)
     ship(LAST, rest)
 
+    for load in loads[5:]:
+        load.wait()
     half[...] = half_matrix(c, half.shape[0], half.shape[1])
     w_in_t[...] = mm_t(half[...], w_in[...]).astype(BF16)
     w_hid_half[...] = mm(half[...], w_hid[...]).astype(BF16)
-    loads[3].wait()
 
     def arrived(k, size):
         block = got.at[k, :, :, 0:size]
@@ -184,7 +196,7 @@
     feat_t[...] = feat[...].T
     grad_feat[...] = jnp.zeros_like(grad_feat)
 
-    def correct(k):
+    def correct(k, unroll=False):
         def piece(j, carry):
             at = pl.multiple_of(k * CHUNK + j * PIECE, 128)
             to = pl.multiple_of(j * PIECE, 128)
@@ -195,7 +207,7 @@
             grad_feat[...] += mm_t(corr, slab)
             return carry
 
-        lax.fori_loop(0, CHUNK // PIECE, piece, 0)
+        lax.fori_loop(0, CHUNK // PIECE, piece, 0, unroll=unroll)
 
     def outer(k):
         def piece(j, carry):
@@ -222,7 +234,7 @@
     slope1_t[...] = silu_slope(pre_t, sig_t)
     lax.fori_loop(3, LAST, turn, 0)
     arrived(LAST, rest)
-    correct(LAST)
+    correct(LAST, unroll=True)
 
     grad[0:256, :] = grad_feat[...].astype(BF16)
     grad_copy = to_twin(grad, 1)
@@ -233,7 +245,21 @@
         back = mm_t(grad[at : at + 256, :], w_out[...]) * slope2[at : at + 256, :]
         back_two[at : at + 256, :] = back.astype(BF16)
 
+    def product(third, lower, part):
+        at = slice(256 * part, 256 * part + 256)
+        if (third, lower) == (0, False):
+            return mm(h2_t[:, at], grad[at, :])
+        if (third, lower) == (2, True):
+            back = mm_t(w_hid_half[...], back_two[at, :]) * slope1_t[:, at]
+            back_one_t[...] = back.astype(BF16)
+            return mm(back_one_t[...], pose[at, :])
+        first_column = 256 * (third - 1) + (768 if lower else 0)
+        return mm(h1_t[:, at], back_two[at, first_column : first_column + 256])
+
     backward(0)
+    for third in range(3):
+        for lower in (False, True):
+            halves[2 * third + lower] = product(third, lower, 0)
     grad_copy.wait_recv()
     backward(1)
 
@@ -254,16 +280,8 @@
 
     copies1 = []
     for third in range(3):
-        if third == 0:
-            upper = mm(h2_t[...], grad[...])
-        else:
-            upper = mm(h1_t[...], back_two[:, 256 * (third - 1) : 256 * third])
-        if third == 2:
-            back = mm_t(w_hid_half[...], back_two[...]) * slope1_t[...]
-            back_one_t[...] = back.astype(BF16)
-            lower = mm(back_one_t[...], pose[...])
-        else:
-            lower = mm(h1_t[...], back_two[:, 512 + 256 * third : 768 + 256 * third])
+        upper = halves[2 * third] + product(third, False, 1)
+        lower = halves[2 * third + 1] + product(third, True, 1)
         both = jnp.concatenate([upper.reshape(64, 8, 256), lower.reshape(64, 8, 256)], axis=1)
         sums0[third] = both.astype(BF16).reshape(4, 4, 4, 16, 256)
         for hop in (1, 3, 2):
@@ -349,12 +367,19 @@
 
 def deliver(head, gb, gwo, gwh, gwi, gb_h, gwo_h, gwh_h, gwi_h, sem):
     width = gb_h.shape[2]
+    step = gb.shape[0] // BLOCKS
     copies = [
-        pltpu.make_async_copy(gb.at[:, head : head + width], gb_h.at[0], sem.at[0]),
-        pltpu.make_async_copy(gwo, gwo_h, sem.at[1]),
-        pltpu.make_async_copy(gwh, gwh_h, sem.at[2]),
-        pltpu.make_async_copy(gwi, gwi_h, sem.at[3]),
+        pltpu.make_async_copy(gwo, gwo_h, sem.at[BLOCKS]),
+        pltpu.make_async_copy(gwh, gwh_h, sem.at[BLOCKS + 1]),
+        pltpu.make_async_copy(gwi, gwi_h, sem.at[BLOCKS + 2]),
     ]
+    for block in range(BLOCKS):
+        here = slice(block * step, block * step + step)
+        copies.append(
+            pltpu.make_async_copy(
+                gb.at[here, head : head + width], gb_h.at[0, here], sem.at[block]
+            )
+        )
     for copy in copies:
         copy.start()
     for copy in copies:
@@ -375,9 +400,14 @@
             pltpu.VMEM((8, hidden), F32),
             pltpu.VMEM((8, p_size), F32),
         ),
-        in_specs=[hbm, hbm, hbm, vmem, vmem, vmem, vmem, vmem],
+        in_specs=[hbm] * 8,
         out_specs=(vmem, vmem, vmem, vmem),
         scratch_shapes=[
+            pltpu.VMEM(w_in.shape, BF16),
+            pltpu.VMEM(w_hid.shape, BF16),
+            pltpu.VMEM(w_out.shape, BF16),
+            pltpu.VMEM((1, frames), jnp.int32),
+            pltpu.VMEM((1, owner.shape[0]), jnp.int32),
             pltpu.VMEM((frames, padded), BF16),
             pltpu.VMEM((p_size, padded), BF16),
             pltpu.VMEM((CHUNKS, 128, 2, CHUNK), BF16),
@@ -396,12 +426,13 @@
             pltpu.VMEM((256, p_size), F32),
             pltpu.VMEM((512, p_size), BF16),
             pltpu.VMEM((512, hidden), BF16),
-            pltpu.VMEM((hidden // 2, 512), BF16),
+            pltpu.VMEM((hidden // 2, 256), BF16),
+            pltpu.VMEM((6, hidden // 2, 256), F32),
             pltpu.VMEM((3, 4, 4, 4, 16, 256), BF16),
             pltpu.VMEM((3, 4, 4, 16, 256), BF16),
             pltpu.VMEM((3, 3, 4, 4, 16, 256), BF16),
             pltpu.VMEM((3, 15, 16, 256), BF16),
-            pltpu.SemaphoreType.DMA((4,)),
+            pltpu.SemaphoreType.DMA((9,)),
             pltpu.SemaphoreType.DMA((CHUNKS,)),
             pltpu.SemaphoreType.DMA((CHUNKS,)),
             pltpu.SemaphoreType.DMA((5, 3)),
@@ -424,7 +455,7 @@
         ),
         in_specs=[hbm] * 4,
         out_specs=(hbm,) * 4,
-        scratch_shapes=[pltpu.SemaphoreType.DMA((4,))],
+        scratch_shapes=[pltpu.SemaphoreType.DMA((BLOCKS + 3,))],
         compiler_params=pltpu.CompilerParams(vmem_limit_bytes=2**20),
     )(*(pltpu.with_memory_space_constraint(value, pltpu.VMEM) for value in kept))
     return gwi.T, gwh, gwo, grad_basis

time: 128 us -> 126 us (0.984)
  Pallas kernels: 127 us -> 125 us
    pallas_call x1, Pallas kernels: 124 us -> 121 us  [on_device(): pl.pallas_call(kernel, out_shape=(pltpu.VMEM((p_size, padded), BF16), plt...]
where the time goes in v3:
time: 126 us; the launch traced here: 125 us
  Pallas kernels  125 us (99%)
    pallas_call x1, Pallas kernels, on_device(): pl.pallas_call(kernel, out_shape=(pltpu.VMEM((p_size, padded), BF16), plt...  121 us
    pallas_call x1, Pallas kernels, on_device(): pl.pallas_call(functools.partial(deliver, p_size), out_shape=(jax.ShapeDt...  3.36 us

profile of v3, /device:TPU:1, one launch (start us, length us, event | category | flops | bytes accessed | tf_op | source)
XLA Modules:
  0.0 125.5 jit_solution(2179516995248102212)
XLA Ops:
  0.6 121.5 %shard_map.111 = (bf16[256,16128]{1,0:T(8,128)(2,1)S(1)}, f32[8,256]{1,0:T(8,128)S(1)}, f32[8,1024]{1,0:T(8,128)S(1)}, f32[8,256]{1,0:T(8,128)S(1)}) custom-call(bf16[128,256]{1,0:T(8,128)(2,1)} %pose_h.1, bf16[128,15744]{1,0:T(8,128)(2,1)} %tgt_h.1, bf16[1,256,15744]{2,1,0:T(8,128)(2,1)} %basis_h.1, bf16[256,1024]{1,0:T(8,128)(2,1)} %w_in_h.1, ...), custom_call_target="tpu_custom_call" | custom-call | tf_op jit(solution)/shard_map/pallas_call | solution.py:395
  122.1 3.4 %shard_map.112 = (bf16[1,256,15744]{2,1,0:T(8,128)(2,1)}, f32[8,256]{1,0:T(8,128)}, f32[8,1024]{1,0:T(8,128)}, f32[8,256]{1,0:T(8,128)}) custom-call(bf16[256,16128]{1,0:T(8,128)(2,1)S(1)} %get-tuple-element.12.gb, f32[8,256]{1,0:T(8,128)S(1)} %get-tuple-element.13.gwo, f32[8,1024]{1,0:T(8,128)S(1)} %get-tuple-element.14.gwh, f32[8,256]{1,0:T(8,128)S(1)} %get-tuple-element.15.gwi), custom_call_target="tpu_custom_call" | custom-call | tf_op jit(solution)/shard_map/pallas_call | solution.py:448

commit v4 on v3

--- a/solution.py
+++ b/solution.py
@@ -65,7 +65,7 @@
     w_in, w_hid, w_out, subject, owner, rows, basis, send, got, pick, feat, feat_t, pose, half, w_in_t, w_hid_half,
     h1_t, h2_t, slope1_t, slope2, grad_feat, grad, back_two, back_one_t,
     halves, sums0, sums1, got1, got2,
-    load_sem, send_sem, got_sem, rs_send, rs_got,
+    load_sem, send_sem, got_sem, rs_send, rs_got, vouched,
 ):
     me = lax.axis_index("dev")
     z, y, x, c = me // 32, (me // 8) % 4, (me // 2) % 4, me % 2
@@ -94,11 +94,28 @@
 
     barrier = pltpu.get_barrier_semaphore()
 
-    def greet(step, carry):
-        pl.semaphore_signal(barrier, inc=1, device_id=(peer(me, step),), device_id_type=MESH)
-        return carry
-
-    lax.fori_loop(1, 128, greet, 0)
+    line, block_of = me % 8, me // 8
+
+    def mate(step):
+        return block_of * 8 + lax.rem(line + step, 8)
+
+    def across(step):
+        return lax.rem(block_of + step, 16) * 8 + line
+
+    def greet_across(step, carry):
+        pl.semaphore_signal(barrier, inc=1, device_id=(across(step),), device_id_type=MESH)
+        return carry
+
+    def greet_mate(step, carry):
+        pl.semaphore_signal(barrier, inc=1, device_id=(mate(step),), device_id_type=MESH)
+        return carry
+
+    def vouch(step, carry):
+        pl.semaphore_signal(vouched, inc=1, device_id=(mate(step),), device_id_type=MESH)
+        return carry
+
+    lax.fori_loop(1, 16, greet_across, 0)
+    lax.fori_loop(1, 8, greet_mate, 0)
     for load in loads[4:]:
         load.start()
 
@@ -120,30 +137,53 @@
 
         lax.fori_loop(0, CHUNK // PIECE, piece, 0)
 
-    def ship(k, size):
+    def ship_to(k, size, to):
+        pltpu.make_async_remote_copy(
+            src_ref=send.at[k, to, :, 0:size],
+            dst_ref=got.at[k, me, :, 0:size],
+            send_sem=send_sem.at[k],
+            recv_sem=got_sem.at[k],
+            device_id=(to,),
+            device_id_type=MESH,
+        ).start()
+
+    def keep(k, size):
         pltpu.make_async_copy(
             send.at[k, me, :, 0:size], got.at[k, me, :, 0:size], got_sem.at[k]
         ).start()
 
+    def ship(k, size):
+        keep(k, size)
+
         def one(step, carry):
-            to = peer(me, step)
-            pltpu.make_async_remote_copy(
-                src_ref=send.at[k, to, :, 0:size],
-                dst_ref=got.at[k, me, :, 0:size],
-                send_sem=send_sem.at[k],
-                recv_sem=got_sem.at[k],
-                device_id=(to,),
-                device_id_type=MESH,
-            ).start()
+            ship_to(k, size, peer(me, step))
             return carry
 
         lax.fori_loop(1, 128, one, 0)
+
+    def first_across(step, carry):
+        ship_to(0, CHUNK, across(lax.rem(step * 4, 15) + 1))
+        return carry
+
+    def first_mate(step, carry):
+        ship_to(0, CHUNK, mate(step))
+        return carry
+
+    def first_others(step, carry):
+        to = lax.rem(block_of + 1 + lax.rem(step, 15), 16) * 8
+        ship_to(0, CHUNK, to + lax.rem(line + 1 + lax.rem(step, 7), 8))
+        return carry
 
     loads[2].wait()
     loads[3].wait()
     fill(0)
-    pl.semaphore_wait(barrier, 127)
-    ship(0, CHUNK)
+    pl.semaphore_wait(barrier, 22)
+    lax.fori_loop(1, 8, vouch, 0)
+    keep(0, CHUNK)
+    lax.fori_loop(0, 15, first_across, 0)
+    lax.fori_loop(1, 8, first_mate, 0)
+    pl.semaphore_wait(vouched, 7)
+    lax.fori_loop(0, 105, first_others, 0)
     loads[4].wait()
 
     def more(k, carry):
@@ -437,6 +477,7 @@
             pltpu.SemaphoreType.DMA((CHUNKS,)),
             pltpu.SemaphoreType.DMA((5, 3)),
             pltpu.SemaphoreType.DMA((5, 3)),
+            pltpu.SemaphoreType.REGULAR,
         ],
         compiler_params=pltpu.CompilerParams(
             collective_id=0, has_side_effects=True, vmem_limit_bytes=VMEM_LIMIT

time: 126 us -> 124 us (0.984)
  Pallas kernels: 125 us -> 123 us
    pallas_call x1, Pallas kernels: 121 us -> 120 us  [on_device(): pl.pallas_call(kernel, out_shape=(pltpu.VMEM((p_size, padded), BF16), plt...]
where the time goes in v4:
time: 124 us
  Pallas kernels  123 us (99%)
    pallas_call x1, Pallas kernels, on_device(): pl.pallas_call(kernel, out_shape=(pltpu.VMEM((p_size, padded), BF16), plt...  120 us
    pallas_call x1, Pallas kernels, on_device(): pl.pallas_call(functools.partial(deliver, p_size), out_shape=(jax.ShapeDt...  3.36 us

profile of v4, /device:TPU:1, one launch (start us, length us, event | category | flops | bytes accessed | tf_op | source)
XLA Modules:
  0.0 123.8 jit_solution(11420824599830513862)
XLA Ops:
  0.6 119.8 %shard_map.111 = (bf16[256,16128]{1,0:T(8,128)(2,1)S(1)}, f32[8,256]{1,0:T(8,128)S(1)}, f32[8,1024]{1,0:T(8,128)S(1)}, f32[8,256]{1,0:T(8,128)S(1)}) custom-call(bf16[128,256]{1,0:T(8,128)(2,1)} %pose_h.1, bf16[128,15744]{1,0:T(8,128)(2,1)} %tgt_h.1, bf16[1,256,15744]{2,1,0:T(8,128)(2,1)} %basis_h.1, bf16[256,1024]{1,0:T(8,128)(2,1)} %w_in_h.1, ...), custom_call_target="tpu_custom_call" | custom-call | tf_op jit(solution)/shard_map/pallas_call | solution.py:435
  120.4 3.4 %shard_map.112 = (bf16[1,256,15744]{2,1,0:T(8,128)(2,1)}, f32[8,256]{1,0:T(8,128)}, f32[8,1024]{1,0:T(8,128)}, f32[8,256]{1,0:T(8,128)}) custom-call(bf16[256,16128]{1,0:T(8,128)(2,1)S(1)} %get-tuple-element.12.gb, f32[8,256]{1,0:T(8,128)S(1)} %get-tuple-element.13.gwo, f32[8,1024]{1,0:T(8,128)S(1)} %get-tuple-element.14.gwh, f32[8,256]{1,0:T(8,128)S(1)} %get-tuple-element.15.gwi), custom_call_target="tpu_custom_call" | custom-call | tf_op jit(solution)/shard_map/pallas_call | solution.py:489

commit v5 on v4

--- a/solution.py
+++ b/solution.py
@@ -116,13 +116,6 @@
 
     lax.fori_loop(1, 16, greet_across, 0)
     lax.fori_loop(1, 8, greet_mate, 0)
-    for load in loads[4:]:
-        load.start()
-
-    rows[:, head + width :] = jnp.zeros((rows.shape[0], rows.shape[1] - head - width), BF16)
-    basis[:, head + width :] = jnp.zeros((basis.shape[0], basis.shape[1] - head - width), BF16)
-    basis[:, 0:head] = jnp.zeros((basis.shape[0], head), BF16)
-    got[LAST, :, :, rest:] = jnp.zeros((128, 2, CHUNK - rest), BF16)
     loads[0].wait()
     loads[1].wait()
     pick[...] = select_matrix(subject[...], owner[...])
@@ -176,6 +169,7 @@
 
     loads[2].wait()
     loads[3].wait()
+    loads[4].start()
     fill(0)
     pl.semaphore_wait(barrier, 22)
     lax.fori_loop(1, 8, vouch, 0)
@@ -184,6 +178,12 @@
     lax.fori_loop(1, 8, first_mate, 0)
     pl.semaphore_wait(vouched, 7)
     lax.fori_loop(0, 105, first_others, 0)
+    for load in loads[5:]:
+        load.start()
+    rows[:, head + width :] = jnp.zeros((rows.shape[0], rows.shape[1] - head - width), BF16)
+    basis[:, head + width :] = jnp.zeros((basis.shape[0], basis.shape[1] - head - width), BF16)
+    basis[:, 0:head] = jnp.zeros((basis.shape[0], head), BF16)
+    got[LAST, :, :, rest:] = jnp.zeros((128, 2, CHUNK - rest), BF16)
     loads[4].wait()
 
     def more(k, carry):
@@ -324,7 +324,7 @@
         lower = halves[2 * third + 1] + product(third, True, 1)
         both = jnp.concatenate([upper.reshape(64, 8, 256), lower.reshape(64, 8, 256)], axis=1)
         sums0[third] = both.astype(BF16).reshape(4, 4, 4, 16, 256)
-        for hop in (1, 3, 2):
+        for hop in (2, 1, 3):
             value = (spots[third] + hop) % 4
             copy = pltpu.make_async_remote_copy(
                 src_ref=rows1(sums0, third, value),

time: 124 us -> 124 us (level)
  no operation moved by 1% of the time
where the time goes in v5:
time: 124 us; the launch traced here: 123 us
  Pallas kernels  123 us (99%)
    pallas_call x1, Pallas kernels, on_device(): pl.pallas_call(kernel, out_shape=(pltpu.VMEM((p_size, padded), BF16), plt...  119 us
    pallas_call x1, Pallas kernels, on_device(): pl.pallas_call(functools.partial(deliver, p_size), out_shape=(jax.ShapeDt...  3.36 us

profile of v5, /device:TPU:1, one launch (start us, length us, event | category | flops | bytes accessed | tf_op | source)
XLA Modules:
  0.0 123.5 jit_solution(17882964300831764385)
XLA Ops:
  0.6 119.5 %shard_map.111 = (bf16[256,16128]{1,0:T(8,128)(2,1)S(1)}, f32[8,256]{1,0:T(8,128)S(1)}, f32[8,1024]{1,0:T(8,128)S(1)}, f32[8,256]{1,0:T(8,128)S(1)}) custom-call(bf16[128,256]{1,0:T(8,128)(2,1)} %pose_h.1, bf16[128,15744]{1,0:T(8,128)(2,1)} %tgt_h.1, bf16[1,256,15744]{2,1,0:T(8,128)(2,1)} %basis_h.1, bf16[256,1024]{1,0:T(8,128)(2,1)} %w_in_h.1, ...), custom_call_target="tpu_custom_call" | custom-call | tf_op jit(solution)/shard_map/pallas_call | solution.py:435
  120.1 3.4 %shard_map.112 = (bf16[1,256,15744]{2,1,0:T(8,128)(2,1)}, f32[8,256]{1,0:T(8,128)}, f32[8,1024]{1,0:T(8,128)}, f32[8,256]{1,0:T(8,128)}) custom-call(bf16[256,16128]{1,0:T(8,128)(2,1)S(1)} %get-tuple-element.12.gb, f32[8,256]{1,0:T(8,128)S(1)} %get-tuple-element.13.gwo, f32[8,1024]{1,0:T(8,128)S(1)} %get-tuple-element.14.gwh, f32[8,256]{1,0:T(8,128)S(1)} %get-tuple-element.15.gwi), custom_call_target="tpu_custom_call" | custom-call | tf_op jit(solution)/shard_map/pallas_call | solution.py:489
